TPU v7x, 512 devices: a whole 4x8x8 slice. The times are simulated.
512 devices in a mesh: gx: 32 (over y, x_hi, core), gz: 16 (over z, x_lo).
Axes of the slice: x: 4 (x_hi: 2, x_lo: 2; x = x_hi * 2 + x_lo), y: 8, z: 8, core: 2. Of those that a mesh axis runs over, the one named last changes fastest.
Arguments:
- multipoles: float32 [81, 64, 32, 2048], P(None, 'gx', None, 'gz')
- kernel_base: float32 [81, 81], replicated, may hold values from -0.625 to 0.625
- kernel_freq: float32 [1025, 81], replicated, may hold values from 0.25 to 2
- res_off: bfloat16 [32, 16, 32, 3, 128], P('gx', 'gz'), may hold values from -0.5 to 0.5
- res_count: int32 [32, 16, 32], P('gx', 'gz'), may hold values from 32 to 128, as said below
- res_scale: float32 [32, 16, 32], P('gx', 'gz'), may hold values from 0.5 to 1
- leave_off: bfloat16 [32, 16, 16, 3, 128], P('gx', 'gz'), may hold values from -0.5 to 0.5
- leave_count: int32 [32, 16, 16], P('gx', 'gz'), may hold values from 32 to 128, as said below
- leave_dest: int32 [32, 16, 16], P('gx', 'gz'), may hold values from 0 to 31
- leave_scale: float32 [32, 16, 16], P('gx', 'gz'), may hold values from 0.5 to 1
- route_blocks: int32 [32, 16, 2, 8], P('gx', 'gz'), may hold values from 0 to 15, as said below
- route_num: int32 [32, 16, 2], P('gx', 'gz'), may hold values from 1 to 8
Outputs:
- taylors: float32 [81, 64, 32, 2048], P(None, 'gx', None, 'gz')
- near_accel: float32 [32, 16, 32, 3, 128], P('gx', 'gz')
Inputs may be any that keep to these rules, and one draw needn't show every extreme that they name: `res_count`: live particles of a block fill its first slots. `leave_count`: live particles of a block fill its first slots. `route_blocks`: row 0 lists the device's leaving blocks bound for the slab at the next lower gx index, row 1 those for the next higher (periodically); the two rows of a device name distinct blocks of its pool; only the first route_num entries of a row are used.
All inputs are finite; a program needn't handle non-finite values.
Results may differ from a plain program's by a relative error of at most 0.0003.
Values may be sent and summed in bfloat16 or wider, within the bound.
A program may use at most 128 MiB of HBM per device.

v0:
```python
import math

import jax
import jax.numpy as jnp
import numpy as np
from jax import lax
from jax.experimental import pallas as pl
from jax.experimental.pallas import tpu as pltpu
from jax.sharding import PartitionSpec as P

softening_sq = 0.04
particle_mass = 1.0 / 128.0
MESH = pl.DeviceIdType.MESH

COMPS = 81
ROWS = 88
SENT = 82
GZ = 16
GX = 32
PLANES = 128
CELLS = 64
HALVES = 9
BLK = 32
POOL = 16
MAXB = 8
TOP = 32700.0
CODE = 128.0
ROOT = math.sqrt(TOP)


def dft_tables():
    r = np.arange(PLANES)
    j = np.arange(PLANES)
    f2 = np.where(j < 64, j, 191 - j)
    angle = 2.0 * np.pi * ((r[:, None] * f2[None, :]) % PLANES) / PLANES
    c, s = np.cos(angle), np.sin(angle)
    forward = np.block([[c, -s], [s, c]])
    inverse = np.block([[c.T, s.T], [-s.T, c.T]])
    turn = 2.0 * np.pi * np.arange(HALVES)[:, None] * r[None, :] / (GZ * PLANES)
    twiddle = np.zeros((2, 16, PLANES))
    twiddle[0, :HALVES] = np.cos(turn)
    twiddle[1, :HALVES] = np.sin(turn)

    def split(table):
        table = table.astype(np.float32)
        high = table.astype(jnp.bfloat16)
        low = (table - high.astype(np.float32)).astype(jnp.bfloat16)
        return [high, low]

    matrices = np.stack(split(forward) + split(inverse))
    return matrices, twiddle.astype(np.float32)


def real_dft(xs):
    n = len(xs)
    if n == 1:
        return [(xs[0], None)]
    even, odd = real_dft(xs[0::2]), real_dft(xs[1::2])
    h = n // 2
    out = [None] * (h + 1)
    out[0] = (even[0][0] + odd[0][0], None)
    out[h] = (even[0][0] - odd[0][0], None)
    for k in range(1, h // 2 + 1):
        if 2 * k == h:
            out[k] = (even[k][0], -odd[k][0])
            continue
        c, s = math.cos(2 * math.pi * k / n), math.sin(2 * math.pi * k / n)
        (er, ei), (orr, oi) = even[k], odd[k]
        tr = orr * c + oi * s
        ti = oi * c - orr * s
        out[k] = (er + tr, ei + ti)
        out[h - k] = (er - tr, ti - ei)
    return out


def real_idft(fs):
    h = len(fs) - 1
    n = 2 * h
    if n == 2:
        return [fs[0][0] + fs[1][0], fs[0][0] - fs[1][0]]
    even, odd = [None] * (h // 2 + 1), [None] * (h // 2 + 1)
    even[0] = (fs[0][0] + fs[h][0], None)
    odd[0] = (fs[0][0] - fs[h][0], None)
    for k in range(1, h // 2 + 1):
        if 2 * k == h:
            even[k] = (2.0 * fs[k][0], None)
            odd[k] = (-2.0 * fs[k][1], None)
            continue
        c, s = math.cos(2 * math.pi * k / n), math.sin(2 * math.pi * k / n)
        (ar, ai), (br, bi) = fs[k], fs[h - k]
        even[k] = (ar + br, ai - bi)
        dr, di = ar - br, ai + bi
        odd[k] = (dr * c - di * s, di * c + dr * s)
    ev, od = real_idft(even), real_idft(odd)
    out = [None] * n
    out[0::2] = ev
    out[1::2] = od
    return out


def split_bf16(x):
    high = x.astype(jnp.bfloat16)
    return high, (x - high.astype(jnp.float32)).astype(jnp.bfloat16)


def dot(a, b):
    return jnp.dot(a, b, preferred_element_type=jnp.float32)


def dot_split(a, b):
    return dot(a[0], b[0]) + (dot(a[1], b[0]) + dot(a[0], b[1]))


def encode(a0, a1):
    diagonal = lax.broadcasted_iota(jnp.int32, a0.shape, 0) == lax.broadcasted_iota(
        jnp.int32, a0.shape, 1
    )

    def one(a):
        largest = jnp.max(jnp.abs(a), axis=1, keepdims=True)
        code = jnp.ceil(jnp.log2(jnp.maximum(largest, 1.2e-38)) * CODE)
        factor = jnp.exp2(code * (-0.5 / CODE)) * ROOT
        return jnp.round(a * factor * factor).astype(jnp.int32), code.astype(jnp.int32)

    q0, c0 = one(a0)
    q1, c1 = one(a1)
    words = (q0 << 16) + q1
    codes = jnp.sum(jnp.where(diagonal, (c0 << 16) + c1, 0), axis=0, keepdims=True)
    return words, codes


def decode(words, codes):
    rows = words.shape[0]
    lane = lax.broadcasted_iota(jnp.int32, (1, 128), 1)
    diagonal = lax.broadcasted_iota(jnp.int32, (rows, 128), 0) == lax.broadcasted_iota(
        jnp.int32, (rows, 128), 1
    )
    c1 = (codes << 16) >> 16
    c0 = (codes - c1) >> 16

    def column(code):
        factor = jnp.exp2(code.astype(jnp.float32) * (0.5 / CODE)) * (1.0 / ROOT)
        factor = jnp.where(lane < COMPS, factor, 0.0)
        return jnp.sum(jnp.where(diagonal, factor, 0.0), axis=1, keepdims=True)

    f0, f1 = column(c0), column(c1)
    low = (words << 16) >> 16
    high = (words - low) >> 16
    return high.astype(jnp.float32) * f0 * f0, low.astype(jnp.float32) * f1 * f1


def kernel(
    mult_hbm,
    base_hbm,
    freq_hbm,
    res_off_hbm,
    leave_off_hbm,
    mats_hbm,
    twid_hbm,
    res_count,
    res_scale,
    leave_count,
    leave_dest,
    leave_scale,
    route_blocks,
    route_num,
    out_hbm,
    near_out,
    in_scr,
    out_scr,
    send_f,
    recv_f,
    send_b,
    recv_b,
    x_scr,
    l_scr,
    y_scr,
    gain_scr,
    base_in,
    base_scr,
    freq_in,
    freq_scr,
    mats,
    twid,
    res_off,
    leave_off,
    pos,
    acc,
    near_tx,
    near_rx,
    in_sem,
    out_sem,
    par_sem,
    fs_sem,
    fr_sem,
    bs_sem,
    br_sem,
    ns_sem,
    nr_sem,
):
    me = lax.axis_index("gz")
    slab = lax.axis_index("gx")
    lower, higher = lax.rem(slab + GX - 1, GX), lax.rem(slab + 1, GX)

    in_copies = [
        pltpu.make_async_copy(
            mult_hbm.at[:, pl.ds(c * 32, 32), :],
            in_scr.reshape(ROWS, CELLS, PLANES).at[pl.ds(0, COMPS), pl.ds(c * 32, 32), :],
            in_sem.at[c],
        )
        for c in range(2)
    ]
    for copy in in_copies:
        copy.start()
    par_copies = [
        pltpu.make_async_copy(src, dst, par_sem.at[i])
        for i, (src, dst) in enumerate(
            [
                (base_hbm, base_in),
                (freq_hbm, freq_in),
                (res_off_hbm, res_off),
                (leave_off_hbm, leave_off),
                (mats_hbm, mats),
                (twid_hbm, twid),
            ]
        )
    ]
    for copy in par_copies:
        copy.start()

    barrier = pltpu.get_barrier_semaphore()

    def greet(s, _):
        pl.semaphore_signal(
            barrier, inc=1, device_id={"gz": lax.rem(me + s, GZ)}, device_id_type=MESH
        )
        return 0

    lax.fori_loop(1, GZ, greet, 0)
    for side in (lower, higher):
        pl.semaphore_signal(barrier, inc=1, device_id={"gx": side}, device_id_type=MESH)

    in_scr[pl.ds(COMPS * CELLS, (ROWS - COMPS) * CELLS), :] = jnp.zeros(
        ((ROWS - COMPS) * CELLS, PLANES), jnp.float32
    )

    def forward_words(c, peer):
        first = c * 32 + 2 * peer
        return encode(
            in_scr[pl.ds(first, ROWS, stride=CELLS), :],
            in_scr[pl.ds(first + 1, ROWS, stride=CELLS), :],
        )

    def copy_f(c, s, sender, receiver):
        return pltpu.make_async_remote_copy(
            src_ref=send_f.at[c, receiver, pl.ds(0, SENT)],
            dst_ref=recv_f.at[c, sender, pl.ds(0, SENT)],
            send_sem=fs_sem.at[c, s],
            recv_sem=fr_sem.at[c, s],
            device_id={"gz": receiver},
            device_id_type=MESH,
        )

    def copy_b(c, s, sender, receiver):
        return pltpu.make_async_remote_copy(
            src_ref=send_b.at[c, receiver, pl.ds(0, SENT)],
            dst_ref=recv_b.at[c, sender, pl.ds(0, SENT)],
            send_sem=bs_sem.at[c, s],
            recv_sem=br_sem.at[c, s],
            device_id={"gz": receiver},
            device_id_type=MESH,
        )

    def put(ref, c, slot, words, codes):
        ref[c, slot, :, :] = words
        ref[c, slot, pl.ds(COMPS, 1), :] = codes

    def peer_after(s):
        return lax.rem(me + s, GZ)

    def peer_before(s):
        return lax.rem(me + GZ - s, GZ)

    def forward_send(c):
        def step(s, _):
            peer = peer_after(s)
            words, codes = forward_words(c, peer)
            put(send_f, c, peer, words, codes)
            copy_f(c, s, me, peer).start()
            return 0

        lax.fori_loop(1, GZ, step, 0)
        words, codes = forward_words(c, me)
        put(recv_f, c, me, words, codes)

    in_copies[0].wait()
    pl.semaphore_wait(barrier, GZ + 1)
    forward_send(0)
    in_copies[1].wait()
    forward_send(1)

    for copy in par_copies:
        copy.wait()
    near_tx[...] = jnp.zeros_like(near_tx)
    lane = lax.broadcasted_iota(jnp.int32, (1, 128), 1)
    for d in range(2):

        def pack(e, _, d=d):
            block = route_blocks[0, 0, d, e]
            scaled = leave_scale[0, 0, block] * leave_off[block].astype(jnp.float32)
            near_tx[d, e, pl.ds(0, 3), :] = scaled.astype(jnp.bfloat16).astype(jnp.float32)
            live = (lane < leave_count[0, 0, block]) & (lane * 0 + e < route_num[0, 0, d])
            near_tx[d, e, pl.ds(3, 1), :] = jnp.where(live, particle_mass, 0.0)
            near_tx[d, e, pl.ds(4, 1), :] = (lane * 0 + leave_dest[0, 0, block]).astype(
                jnp.float32
            )
            return 0

        lax.fori_loop(0, MAXB, pack, 0)

    def copy_n(d):
        return pltpu.make_async_remote_copy(
            src_ref=near_tx.at[d],
            dst_ref=near_rx.at[pl.ds(MAXB * (1 - d), MAXB)],
            send_sem=ns_sem.at[d],
            recv_sem=nr_sem.at[d],
            device_id={"gx": higher if d == 1 else lower},
            device_id_type=MESH,
        )

    for d in range(2):
        copy_n(d).start()

    base_scr[...] = jnp.zeros_like(base_scr)
    base_scr[pl.ds(0, COMPS), pl.ds(0, COMPS)] = base_in[...]
    y_scr[...] = jnp.zeros_like(y_scr)
    freq_scr[...] = jnp.zeros_like(freq_scr)
    freq_scr[pl.ds(0, 1025), pl.ds(0, COMPS)] = freq_in[...]
    for f1 in range(HALVES):
        rows = jnp.concatenate(
            [
                freq_scr[pl.ds(f1, 64, stride=GZ), :],
                freq_scr[pl.ds(GZ - f1, 64, stride=GZ), :],
            ],
            axis=0,
        )
        gain_scr[f1] = jnp.transpose(rows)[0:ROWS] * (1.0 / (GZ * PLANES))

    row3 = lax.broadcasted_iota(jnp.int32, (3, 128), 0)
    sub8 = lax.broadcasted_iota(jnp.int32, (8, 128), 0)
    pos[...] = jnp.zeros_like(pos)
    acc[...] = jnp.zeros_like(acc)

    def place(b, _):
        centre = jnp.where(row3 == 1, b, 0).astype(jnp.float32)
        pos[b + 1, pl.ds(0, 3), :] = (
            res_scale[0, 0, b] * res_off[b].astype(jnp.float32) + centre
        )
        return 0

    lax.fori_loop(0, BLK, place, 0)

    def pull(sinks, source_t, mass_of):
        rows = [[jnp.broadcast_to(p[i : i + 1, :], (8, 128)) for i in range(3)] for p in sinks]
        sums = [[jnp.zeros((8, 128), jnp.float32) for _ in range(3)] for _ in sinks]
        for g in range(16):
            part = source_t[8 * g : 8 * g + 8, :]
            q = [jnp.broadcast_to(part[:, i : i + 1], (8, 128)) for i in range(3)]
            mass = mass_of(g, part)
            for n, p in enumerate(rows):
                d = [q[i] - p[i] for i in range(3)]
                square = d[0] * d[0] + d[1] * d[1] + d[2] * d[2] + softening_sq
                inverse = lax.rsqrt(square)
                weight = mass * inverse * inverse * inverse
                for i in range(3):
                    sums[n][i] = sums[n][i] + d[i] * weight
        return sums

    def resident(b, _):
        count = res_count[0, 0, b]
        source_t = jnp.transpose(pos[b + 1])

        def mass_of(g, part):
            return jnp.where(sub8 + 8 * g < count, particle_mass, 0.0)

        sums = pull([pos[b], pos[b + 1], pos[b + 2]], source_t, mass_of)
        for n in range(3):
            for i in range(3):
                acc[b + n, i] = acc[b + n, i] + sums[n][i]
        return 0

    lax.fori_loop(0, BLK, resident, 0)

    def stack3(sums):
        out = jnp.zeros((8, 128), jnp.float32)
        for i in range(3):
            total = jnp.sum(sums[i], axis=0, keepdims=True)
            out = jnp.where(sub8 == i, jnp.broadcast_to(total, (8, 128)), out)
        return out

    def settle(b, _):
        near_out[b] = stack3([acc[b + 1, i] for i in range(3)])
        return 0

    lax.fori_loop(0, BLK, settle, 0)

    def arrivals():
        for d in range(2):
            copy_n(d).wait()

        def arrival(a, _):
            block = near_rx[a]
            target = jnp.broadcast_to(block[4:5, :], (8, 128))
            sink = jnp.zeros((8, 128), jnp.float32)
            for b in range(BLK):
                sink = sink + jnp.where(target == float(b), pos[b + 1], 0.0)
            source_t = jnp.transpose(block + jnp.where(sub8 == 1, target, 0.0))

            def mass_of(g, part):
                return jnp.broadcast_to(part[:, 3:4], (8, 128))

            pulled = stack3(pull([sink], source_t, mass_of)[0])
            for b in range(BLK):
                near_out[b] = near_out[b] + jnp.where(target == float(b), pulled, 0.0)
            return 0

        lax.fori_loop(0, 2 * MAXB, arrival, 0)

    def open_pencil(c, sender):
        words = recv_f[c, sender]
        a0, a1 = decode(words, recv_f[c, sender, pl.ds(COMPS, 1), :])
        x_scr[0, sender] = a0
        x_scr[1, sender] = a1

    def pencils(c):
        open_pencil(c, me)

        def take(s, _):
            sender = peer_before(s)
            copy_f(c, s, sender, me).wait_recv()
            open_pencil(c, sender)
            return 0

        lax.fori_loop(1, GZ, take, 0)

        def spread(i, _):
            col, tile = i // 11, pl.multiple_of((i % 11) * 8, 8)
            found = real_dft([x_scr[col, d, pl.ds(tile, 8), :] for d in range(GZ)])
            for f1 in range(HALVES):
                re, im = found[f1]
                cos = jnp.broadcast_to(twid[0, f1 : f1 + 1, :], (8, 128))
                sin = jnp.broadcast_to(twid[1, f1 : f1 + 1, :], (8, 128))
                if f1 == 0:
                    out = (re, jnp.zeros_like(re))
                elif im is None:
                    out = (re * cos, -re * sin)
                else:
                    out = (re * cos + im * sin, im * cos - re * sin)
                l_scr[f1, col, pl.ds(tile, 8), pl.ds(0, 128)] = out[0]
                l_scr[f1, col, pl.ds(tile, 8), pl.ds(128, 128)] = out[1]
            return 0

        lax.fori_loop(0, 22, spread, 0)

        def convolve(g, _):
            at = pl.ds(g * 3, 3)
            spec = dot_split(
                split_bf16(l_scr[at].reshape(6 * ROWS, 256)), (mats[0], mats[1])
            ).reshape(3, 2, ROWS, 256)
            gain = gain_scr[at]
            gain = jnp.concatenate([gain, gain], axis=2)[:, None]
            back = dot_split(
                split_bf16((spec * gain).reshape(6 * ROWS, 256)), (mats[2], mats[3])
            )
            l_scr[at] = back.reshape(3, 2, ROWS, 256)
            return 0

        lax.fori_loop(0, 3, convolve, 0)

        def gather(i, _):
            col, tile = i // 11, pl.multiple_of((i % 11) * 8, 8)
            freqs = []
            for f1 in range(HALVES):
                re = l_scr[f1, col, pl.ds(tile, 8), pl.ds(0, 128)]
                if f1 == 0:
                    freqs.append((re, None))
                    continue
                im = l_scr[f1, col, pl.ds(tile, 8), pl.ds(128, 128)]
                cos = jnp.broadcast_to(twid[0, f1 : f1 + 1, :], (8, 128))
                sin = jnp.broadcast_to(twid[1, f1 : f1 + 1, :], (8, 128))
                if f1 == HALVES - 1:
                    freqs.append((re * cos - im * sin, None))
                else:
                    freqs.append((re * cos - im * sin, im * cos + re * sin))
            for d, value in enumerate(real_idft(freqs)):
                y_scr[d, col, pl.ds(tile, 8), :] = value
            return 0

        lax.fori_loop(0, 22, gather, 0)

        base = split_bf16(base_scr[...])

        def mixed_words(d):
            both = jnp.concatenate([y_scr[d, 0], y_scr[d, 1]], axis=1)
            mixed = dot_split(base, split_bf16(both))
            return encode(mixed[:, 0:128], mixed[:, 128:256])

        def answer(s, _):
            peer = peer_after(s)
            words, codes = mixed_words(peer)
            put(send_b, c, peer, words, codes)
            copy_b(c, s, me, peer).start()
            return 0

        lax.fori_loop(1, GZ, answer, 0)
        words, codes = mixed_words(me)
        put(recv_b, c, me, words, codes)

    def close_pencil(c, sender):
        words = recv_b[c, sender]
        a0, a1 = decode(words, recv_b[c, sender, pl.ds(COMPS, 1), :])
        first = c * 32 + 2 * sender
        out_scr[pl.ds(first, ROWS, stride=CELLS), :] = a0
        out_scr[pl.ds(first + 1, ROWS, stride=CELLS), :] = a1

    def out_copy(c):
        return pltpu.make_async_copy(
            out_scr.reshape(ROWS, CELLS, PLANES).at[pl.ds(0, COMPS), pl.ds(c * 32, 32), :],
            out_hbm.at[:, pl.ds(c * 32, 32), :],
            out_sem.at[c],
        )

    def results(c):
        close_pencil(c, me)

        def take(s, _):
            sender = peer_before(s)
            copy_b(c, s, sender, me).wait_recv()
            close_pencil(c, sender)
            return 0

        lax.fori_loop(1, GZ, take, 0)
        out_copy(c).start()

    pencils(0)
    arrivals()
    pencils(1)
    results(0)
    results(1)

    def drain(s, _):
        for c in range(2):
            copy_f(c, s, me, peer_after(s)).wait_send()
            copy_b(c, s, me, peer_after(s)).wait_send()
        return 0

    lax.fori_loop(1, GZ, drain, 0)
    for c in range(2):
        out_copy(c).wait()


def on_device(
    multipoles,
    kernel_base,
    kernel_freq,
    res_off,
    res_count,
    res_scale,
    leave_off,
    leave_count,
    leave_dest,
    leave_scale,
    route_blocks,
    route_num,
):
    matrices, twiddle = dft_tables()
    anywhere = pl.BlockSpec(memory_space=pl.ANY)
    smem = pl.BlockSpec(memory_space=pltpu.SMEM)
    vmem = pl.BlockSpec(memory_space=pltpu.VMEM)
    f32, i32 = jnp.float32, jnp.int32
    dma = pltpu.SemaphoreType.DMA
    taylors, near = pl.pallas_call(
        kernel,
        out_shape=(
            jax.ShapeDtypeStruct((COMPS, CELLS, PLANES), f32),
            jax.ShapeDtypeStruct((BLK, 8, 128), f32),
        ),
        in_specs=[anywhere] * 7 + [smem] * 7,
        out_specs=(anywhere, vmem),
        scratch_shapes=[
            pltpu.VMEM((ROWS * CELLS, PLANES), f32),
            pltpu.VMEM((ROWS * CELLS, PLANES), f32),
            pltpu.VMEM((2, GZ, ROWS, 128), i32),
            pltpu.VMEM((2, GZ, ROWS, 128), i32),
            pltpu.VMEM((2, GZ, ROWS, 128), i32),
            pltpu.VMEM((2, GZ, ROWS, 128), i32),
            pltpu.VMEM((2, GZ, ROWS, 128), f32),
            pltpu.VMEM((HALVES, 2, ROWS, 256), f32),
            pltpu.VMEM((GZ, 2, 128, 128), f32),
            pltpu.VMEM((HALVES, ROWS, 128), f32),
            pltpu.VMEM((COMPS, COMPS), f32),
            pltpu.VMEM((ROWS, 128), f32),
            pltpu.VMEM((1025, COMPS), f32),
            pltpu.VMEM((1040, 128), f32),
            pltpu.VMEM((4, 256, 256), jnp.bfloat16),
            pltpu.VMEM((2, 16, 128), f32),
            pltpu.VMEM((BLK, 3, 128), jnp.bfloat16),
            pltpu.VMEM((POOL, 3, 128), jnp.bfloat16),
            pltpu.VMEM((BLK + 2, 8, 128), f32),
            pltpu.VMEM((BLK + 2, 3, 8, 128), f32),
            pltpu.VMEM((2, MAXB, 8, 128), f32),
            pltpu.VMEM((2 * MAXB, 8, 128), f32),
            dma((2,)),
            dma((2,)),
            dma((6,)),
            dma((2, GZ)),
            dma((2, GZ)),
            dma((2, GZ)),
            dma((2, GZ)),
            dma((2,)),
            dma((2,)),
        ],
        compiler_params=pltpu.CompilerParams(
            collective_id=0, has_side_effects=True, vmem_limit_bytes=48 * 2**20
        ),
    )(
        multipoles.reshape(COMPS, CELLS, PLANES),
        kernel_base,
        kernel_freq,
        res_off[0, 0],
        leave_off[0, 0],
        jnp.asarray(matrices),
        jnp.asarray(twiddle),
        res_count,
        res_scale,
        leave_count,
        leave_dest,
        leave_scale,
        route_blocks,
        route_num,
    )
    return (taylors.reshape(multipoles.shape), near[:, 0:3][None, None])


def solution(mesh):
    in_specs = (
        P(None, "gx", None, "gz"),
        P(),
        P(),
        P("gx", "gz", None, None, None),
        P("gx", "gz", None),
        P("gx", "gz", None),
        P("gx", "gz", None, None, None),
        P("gx", "gz", None),
        P("gx", "gz", None),
        P("gx", "gz", None),
        P("gx", "gz", None, None),
        P("gx", "gz", None),
    )
    out_specs = (P(None, "gx", None, "gz"), P("gx", "gz", None, None, None))
    return jax.shard_map(
        on_device, mesh=mesh, in_specs=in_specs, out_specs=out_specs, check_vma=False
    )
```

profile of v0, /device:TPU:31, one launch (start us, length us, event | category | flops | bytes accessed | tf_op | source)
XLA Modules:
  0.0 87.5 jit_solution(4259773197452700765)
XLA Ops:
  0.6 0.7 copy.23
  1.3 0.8 copy.22
  2.1 1.2 %copy.18.freq_hbm = f32[1025,81]{1,0:T(8,128)S(1)} copy(f32[1025,81]{0,1:T(8,128)} %param.16) | data formatting | bytes 664200 | tf_op args[2]
  3.3 0.0 copy-start
  3.3 1.0 %copy-done = bf16[4,256,256]{2,1,0:T(8,128)(2,1)S(1)} copy-done((bf16[4,256,256]{2,1,0:T(8,128)(2,1)S(1)}, bf16[4,256,256]{2,1,0:T(8,128)(2,1)}, u32[]{:S(2)}) %copy-start) | copy-done | bytes 524312
  4.4 0.0 copy-start.1
  4.4 0.8 copy-done.1
  5.2 0.0 copy-start.2
  5.2 0.7 copy-done.2
  5.9 0.0 copy-start.3
  5.9 0.7 copy-done.3
  6.6 0.0 copy-start.4
  6.6 0.7 copy-done.4
  7.2 0.0 copy-start.5
  7.2 0.7 copy-done.5
  7.9 0.0 copy-start.6
  7.9 0.7 copy-done.6
  8.5 0.0 copy-start.7
  8.5 0.7 copy-done.7
  9.2 0.0 copy-start.8
  9.2 0.7 copy-done.8
  9.8 0.0 copy-start.9
  9.8 0.7 copy-done.9
  10.5 74.9 %shard_map.149 = (f32[81,64,128]{2,1,0:T(8,128)S(1)}, f32[32,8,128]{2,1,0:T(8,128)S(1)}) custom-call(f32[81,64,128]{2,1,0:T(8,128)} %bitcast.13, f32[81,81]{1,0:T(8,128)S(1)} %copy-done.1, f32[1025,81]{1,0:T(8,128)S(1)} %copy.18.freq_hbm, bf16[32,3,128]{2,1,0:T(4,128)(2,1)S(1)} %bitcast.11, bf16[16,3,128]{2,1,0:T(4,128)(2,1)S(1)} %bitcast.12, ...), custom_call_target="tpu_custom_call" | custom-call | tf_op jit(solution)/shard_map/pallas_call | solution.py:582
  85.4 0.6 copy.19
  86.0 1.5 %copy.25 = f32[81,2,32,128]{3,2,1,0:T(8,128)} copy(f32[81,2,32,128]{3,2,1,0:T(8,128)S(1)} %bitcast.10) | data formatting | bytes 5308416
  (1 shorter events, 0.0 us)
Async XLA Ops:
  3.3 1.0 %copy-start = (bf16[4,256,256]{2,1,0:T(8,128)(2,1)S(1)}, bf16[4,256,256]{2,1,0:T(8,128)(2,1)}, u32[]{:S(2)}) copy-start(bf16[4,256,256]{2,1,0:T(8,128)(2,1)} %constant.4.clone.mats_hbm) | copy-start | bytes 1572868
  4.4 0.8 copy-start.1
  5.2 0.7 copy-start.2
  5.9 0.7 copy-start.3
  6.6 0.7 copy-start.4
  7.2 0.7 copy-start.5
  7.9 0.7 copy-start.6
  8.5 0.7 copy-start.7
  9.2 0.7 copy-start.8
  9.8 0.7 copy-start.9
where the time goes:
time: 88 us; the launch traced here: 87.5 us
  Pallas kernels  74.9 us (85%)
  local copies, waits for them, and re-layouts  12 us (14%)
    pallas_call x1, Pallas kernels, on_device(): pl.pallas_call(kernel, out_shape=(jax.ShapeDtypeStruct((COMPS, CELLS, PLA...  74.9 us
    unnamed x25, local copies, waits for them, and re-layouts  12 us

commit v1 on v0

--- a/solution.py
+++ b/solution.py
@@ -40,15 +40,7 @@
     twiddle = np.zeros((2, 16, PLANES))
     twiddle[0, :HALVES] = np.cos(turn)
     twiddle[1, :HALVES] = np.sin(turn)
-
-    def split(table):
-        table = table.astype(np.float32)
-        high = table.astype(jnp.bfloat16)
-        low = (table - high.astype(np.float32)).astype(jnp.bfloat16)
-        return [high, low]
-
-    matrices = np.stack(split(forward) + split(inverse))
-    return matrices, twiddle.astype(np.float32)
+    return np.stack([forward, inverse]).astype(np.float32), twiddle.astype(np.float32)
 
 
 def real_dft(xs):
@@ -157,17 +149,16 @@
     leave_off_hbm,
     mats_hbm,
     twid_hbm,
-    res_count,
-    res_scale,
-    leave_count,
-    leave_dest,
-    leave_scale,
-    route_blocks,
-    route_num,
-    out_hbm,
+    res_count_hbm,
+    res_scale_hbm,
+    leave_count_hbm,
+    leave_dest_hbm,
+    leave_scale_hbm,
+    route_blocks_hbm,
+    route_num_hbm,
+    out,
     near_out,
     in_scr,
-    out_scr,
     send_f,
     recv_f,
     send_b,
@@ -180,16 +171,25 @@
     base_scr,
     freq_in,
     freq_scr,
+    mats_in,
     mats,
     twid,
     res_off,
     leave_off,
-    pos,
+    res_count,
+    res_scale,
+    leave_count,
+    leave_dest,
+    leave_scale,
+    route_blocks,
+    route_num,
+    leave_rows,
+    pos_rows,
     acc,
+    near,
     near_tx,
     near_rx,
     in_sem,
-    out_sem,
     par_sem,
     fs_sem,
     fr_sem,
@@ -212,6 +212,18 @@
     ]
     for copy in in_copies:
         copy.start()
+    barrier = pltpu.get_barrier_semaphore()
+
+    def greet(s, _):
+        pl.semaphore_signal(
+            barrier, inc=1, device_id={"gz": lax.rem(me + s, GZ)}, device_id_type=MESH
+        )
+        return 0
+
+    lax.fori_loop(1, GZ, greet, 0)
+    for side in (lower, higher):
+        pl.semaphore_signal(barrier, inc=1, device_id={"gx": side}, device_id_type=MESH)
+
     par_copies = [
         pltpu.make_async_copy(src, dst, par_sem.at[i])
         for i, (src, dst) in enumerate(
@@ -220,25 +232,20 @@
                 (freq_hbm, freq_in),
                 (res_off_hbm, res_off),
                 (leave_off_hbm, leave_off),
-                (mats_hbm, mats),
+                (mats_hbm, mats_in),
                 (twid_hbm, twid),
+                (res_count_hbm, res_count),
+                (res_scale_hbm, res_scale),
+                (leave_count_hbm, leave_count),
+                (leave_dest_hbm, leave_dest),
+                (leave_scale_hbm, leave_scale),
+                (route_blocks_hbm, route_blocks),
+                (route_num_hbm, route_num),
             ]
         )
     ]
     for copy in par_copies:
         copy.start()
-
-    barrier = pltpu.get_barrier_semaphore()
-
-    def greet(s, _):
-        pl.semaphore_signal(
-            barrier, inc=1, device_id={"gz": lax.rem(me + s, GZ)}, device_id_type=MESH
-        )
-        return 0
-
-    lax.fori_loop(1, GZ, greet, 0)
-    for side in (lower, higher):
-        pl.semaphore_signal(barrier, inc=1, device_id={"gx": side}, device_id_type=MESH)
 
     in_scr[pl.ds(COMPS * CELLS, (ROWS - COMPS) * CELLS), :] = jnp.zeros(
         ((ROWS - COMPS) * CELLS, PLANES), jnp.float32
@@ -302,12 +309,16 @@
     for copy in par_copies:
         copy.wait()
     near_tx[...] = jnp.zeros_like(near_tx)
+    for i in range(3):
+        leave_rows.reshape(POOL * 8, 128)[pl.ds(i, POOL, stride=8), :] = leave_off[i].astype(
+            jnp.float32
+        )
     lane = lax.broadcasted_iota(jnp.int32, (1, 128), 1)
     for d in range(2):
 
         def pack(e, _, d=d):
             block = route_blocks[0, 0, d, e]
-            scaled = leave_scale[0, 0, block] * leave_off[block].astype(jnp.float32)
+            scaled = leave_scale[0, 0, block] * leave_rows[block][0:3]
             near_tx[d, e, pl.ds(0, 3), :] = scaled.astype(jnp.bfloat16).astype(jnp.float32)
             live = (lane < leave_count[0, 0, block]) & (lane * 0 + e < route_num[0, 0, d])
             near_tx[d, e, pl.ds(3, 1), :] = jnp.where(live, particle_mass, 0.0)
@@ -331,11 +342,19 @@
     for d in range(2):
         copy_n(d).start()
 
+    for i in range(2):
+        mats[2 * i], mats[2 * i + 1] = split_bf16(mats_in[i])
     base_scr[...] = jnp.zeros_like(base_scr)
     base_scr[pl.ds(0, COMPS), pl.ds(0, COMPS)] = base_in[...]
     y_scr[...] = jnp.zeros_like(y_scr)
     freq_scr[...] = jnp.zeros_like(freq_scr)
-    freq_scr[pl.ds(0, 1025), pl.ds(0, COMPS)] = freq_in[...]
+    for i in range(8):
+        part = freq_in[:, i * 128 : i * 128 + 128]
+        part = jnp.concatenate([part, jnp.zeros((128 - COMPS, 128), jnp.float32)], axis=0)
+        freq_scr[pl.ds(i * 128, 128), :] = jnp.transpose(part)
+    last = jnp.broadcast_to(freq_in[:, 1024:1025], (COMPS, 128))
+    last = jnp.concatenate([last, jnp.zeros((128 - COMPS, 128), jnp.float32)], axis=0)
+    freq_scr[pl.ds(1024, 1), :] = jnp.transpose(last)[0:1]
     for f1 in range(HALVES):
         rows = jnp.concatenate(
             [
@@ -346,16 +365,16 @@
         )
         gain_scr[f1] = jnp.transpose(rows)[0:ROWS] * (1.0 / (GZ * PLANES))
 
-    row3 = lax.broadcasted_iota(jnp.int32, (3, 128), 0)
     sub8 = lax.broadcasted_iota(jnp.int32, (8, 128), 0)
-    pos[...] = jnp.zeros_like(pos)
+    pos_rows[...] = jnp.zeros_like(pos_rows)
+    pos = pos_rows.reshape(BLK + 2, 8, 128)
     acc[...] = jnp.zeros_like(acc)
+    for i in range(3):
+        pos_rows[pl.ds(8 + i, BLK, stride=8), :] = res_off[i].astype(jnp.float32)
 
     def place(b, _):
-        centre = jnp.where(row3 == 1, b, 0).astype(jnp.float32)
-        pos[b + 1, pl.ds(0, 3), :] = (
-            res_scale[0, 0, b] * res_off[b].astype(jnp.float32) + centre
-        )
+        centre = jnp.where(sub8 == 1, b, 0).astype(jnp.float32)
+        pos[b + 1] = res_scale[0, 0, b] * pos[b + 1] + centre
         return 0
 
     lax.fori_loop(0, BLK, place, 0)
@@ -399,7 +418,7 @@
         return out
 
     def settle(b, _):
-        near_out[b] = stack3([acc[b + 1, i] for i in range(3)])
+        near[pl.ds(pl.multiple_of(b * 8, 8), 8), :] = stack3([acc[b + 1, i] for i in range(3)])
         return 0
 
     lax.fori_loop(0, BLK, settle, 0)
@@ -421,10 +440,13 @@
 
             pulled = stack3(pull([sink], source_t, mass_of)[0])
             for b in range(BLK):
-                near_out[b] = near_out[b] + jnp.where(target == float(b), pulled, 0.0)
+                at = pl.ds(b * 8, 8)
+                near[at, :] = near[at, :] + jnp.where(target == float(b), pulled, 0.0)
             return 0
 
         lax.fori_loop(0, 2 * MAXB, arrival, 0)
+        for i in range(3):
+            near_out[i] = near[pl.ds(i, BLK, stride=8), :]
 
     def open_pencil(c, sender):
         words = recv_f[c, sender]
@@ -520,15 +542,8 @@
         words = recv_b[c, sender]
         a0, a1 = decode(words, recv_b[c, sender, pl.ds(COMPS, 1), :])
         first = c * 32 + 2 * sender
-        out_scr[pl.ds(first, ROWS, stride=CELLS), :] = a0
-        out_scr[pl.ds(first + 1, ROWS, stride=CELLS), :] = a1
-
-    def out_copy(c):
-        return pltpu.make_async_copy(
-            out_scr.reshape(ROWS, CELLS, PLANES).at[pl.ds(0, COMPS), pl.ds(c * 32, 32), :],
-            out_hbm.at[:, pl.ds(c * 32, 32), :],
-            out_sem.at[c],
-        )
+        out[pl.ds(first, COMPS, stride=CELLS), :] = a0[0:COMPS]
+        out[pl.ds(first + 1, COMPS, stride=CELLS), :] = a1[0:COMPS]
 
     def results(c):
         close_pencil(c, me)
@@ -540,7 +555,6 @@
             return 0
 
         lax.fori_loop(1, GZ, take, 0)
-        out_copy(c).start()
 
     pencils(0)
     arrivals()
@@ -555,8 +569,18 @@
         return 0
 
     lax.fori_loop(1, GZ, drain, 0)
-    for c in range(2):
-        out_copy(c).wait()
+
+
+def write_out(far, near, far_hbm, near_hbm, sem):
+    copies = [pltpu.make_async_copy(near, near_hbm, sem.at[9])]
+    size = COMPS * CELLS // 9
+    for i in range(9):
+        part = pl.ds(i * size, size)
+        copies.append(pltpu.make_async_copy(far.at[part], far_hbm.at[part], sem.at[i]))
+    for copy in copies:
+        copy.start()
+    for copy in copies:
+        copy.wait()
 
 
 def on_device(
@@ -574,21 +598,36 @@
     route_num,
 ):
     matrices, twiddle = dft_tables()
-    anywhere = pl.BlockSpec(memory_space=pl.ANY)
-    smem = pl.BlockSpec(memory_space=pltpu.SMEM)
+    hbm = pl.BlockSpec(memory_space=pltpu.HBM)
     vmem = pl.BlockSpec(memory_space=pltpu.VMEM)
     f32, i32 = jnp.float32, jnp.int32
     dma = pltpu.SemaphoreType.DMA
+    operands = [
+        multipoles.reshape(COMPS, CELLS, PLANES),
+        kernel_base,
+        jnp.transpose(kernel_freq),
+        jnp.transpose(res_off[0, 0], (1, 0, 2)),
+        jnp.transpose(leave_off[0, 0], (1, 0, 2)),
+        jnp.asarray(matrices),
+        jnp.asarray(twiddle),
+        res_count,
+        res_scale,
+        leave_count,
+        leave_dest,
+        leave_scale,
+        route_blocks,
+        route_num,
+    ]
+    operands = [pltpu.with_memory_space_constraint(x, pltpu.HBM) for x in operands]
     taylors, near = pl.pallas_call(
         kernel,
         out_shape=(
-            jax.ShapeDtypeStruct((COMPS, CELLS, PLANES), f32),
-            jax.ShapeDtypeStruct((BLK, 8, 128), f32),
+            pltpu.VMEM((COMPS * CELLS, PLANES), f32),
+            pltpu.VMEM((3, BLK, 128), f32),
         ),
-        in_specs=[anywhere] * 7 + [smem] * 7,
-        out_specs=(anywhere, vmem),
+        in_specs=[hbm] * 14,
+        out_specs=(vmem, vmem),
         scratch_shapes=[
-            pltpu.VMEM((ROWS * CELLS, PLANES), f32),
             pltpu.VMEM((ROWS * CELLS, PLANES), f32),
             pltpu.VMEM((2, GZ, ROWS, 128), i32),
             pltpu.VMEM((2, GZ, ROWS, 128), i32),
@@ -600,19 +639,28 @@
             pltpu.VMEM((HALVES, ROWS, 128), f32),
             pltpu.VMEM((COMPS, COMPS), f32),
             pltpu.VMEM((ROWS, 128), f32),
-            pltpu.VMEM((1025, COMPS), f32),
+            pltpu.VMEM((COMPS, 1025), f32),
             pltpu.VMEM((1040, 128), f32),
+            pltpu.VMEM((2, 256, 256), f32),
             pltpu.VMEM((4, 256, 256), jnp.bfloat16),
             pltpu.VMEM((2, 16, 128), f32),
-            pltpu.VMEM((BLK, 3, 128), jnp.bfloat16),
-            pltpu.VMEM((POOL, 3, 128), jnp.bfloat16),
-            pltpu.VMEM((BLK + 2, 8, 128), f32),
+            pltpu.VMEM((3, BLK, 128), jnp.bfloat16),
+            pltpu.VMEM((3, POOL, 128), jnp.bfloat16),
+            pltpu.SMEM((1, 1, BLK), i32),
+            pltpu.SMEM((1, 1, BLK), f32),
+            pltpu.SMEM((1, 1, POOL), i32),
+            pltpu.SMEM((1, 1, POOL), i32),
+            pltpu.SMEM((1, 1, POOL), f32),
+            pltpu.SMEM((1, 1, 2, MAXB), i32),
+            pltpu.SMEM((1, 1, 2), i32),
+            pltpu.VMEM((POOL, 8, 128), f32),
+            pltpu.VMEM(((BLK + 2) * 8, 128), f32),
             pltpu.VMEM((BLK + 2, 3, 8, 128), f32),
+            pltpu.VMEM((BLK * 8, 128), f32),
             pltpu.VMEM((2, MAXB, 8, 128), f32),
             pltpu.VMEM((2 * MAXB, 8, 128), f32),
             dma((2,)),
-            dma((2,)),
-            dma((6,)),
+            dma((13,)),
             dma((2, GZ)),
             dma((2, GZ)),
             dma((2, GZ)),
@@ -621,25 +669,20 @@
             dma((2,)),
         ],
         compiler_params=pltpu.CompilerParams(
-            collective_id=0, has_side_effects=True, vmem_limit_bytes=48 * 2**20
+            collective_id=0, has_side_effects=True, vmem_limit_bytes=40 * 2**20
         ),
-    )(
-        multipoles.reshape(COMPS, CELLS, PLANES),
-        kernel_base,
-        kernel_freq,
-        res_off[0, 0],
-        leave_off[0, 0],
-        jnp.asarray(matrices),
-        jnp.asarray(twiddle),
-        res_count,
-        res_scale,
-        leave_count,
-        leave_dest,
-        leave_scale,
-        route_blocks,
-        route_num,
-    )
-    return (taylors.reshape(multipoles.shape), near[:, 0:3][None, None])
+    )(*operands)
+    taylors, near = pl.pallas_call(
+        write_out,
+        out_shape=(
+            pltpu.HBM((COMPS * CELLS, PLANES), f32),
+            pltpu.HBM((3, BLK, 128), f32),
+        ),
+        in_specs=[vmem] * 2,
+        out_specs=(hbm, hbm),
+        scratch_shapes=[dma((10,))],
+    )(*[pltpu.with_memory_space_constraint(x, pltpu.VMEM) for x in (taylors, near)])
+    return (taylors.reshape(multipoles.shape), jnp.transpose(near, (1, 0, 2))[None, None])
 
 
 def solution(mesh):

time: 88 us -> 76 us (0.86)
  local copies, waits for them, and re-layouts: 12 us -> 0 us
    unnamed x25 -> x0, local copies, waits for them, and re-layouts: 12 us -> none
    pallas_call x1 -> x2, Pallas kernels: 74.9 us -> 75.3 us  [the longest x1 73.7 us: on_device(): pl.pallas_call(kernel, out_shape=(pltpu.VMEM((COMPS * CELLS, PLANES), f32...]
where the time goes in v1:
time: 76 us; the launch traced here: 75.9 us
  Pallas kernels  75.3 us (99%)
    pallas_call x1, Pallas kernels, on_device(): pl.pallas_call(kernel, out_shape=(pltpu.VMEM((COMPS * CELLS, PLANES), f32...  73.7 us
    pallas_call x1, Pallas kernels, on_device(): pl.pallas_call(write_out, out_shape=(pltpu.HBM((COMPS * CELLS, PLANES), f...  1.6 us

profile of v1, /device:TPU:31, one launch (start us, length us, event | category | flops | bytes accessed | tf_op | source)
XLA Modules:
  0.0 75.9 jit_solution(11837157891950491868)
XLA Ops:
  0.6 73.7 %shard_map.149 = (f32[5184,128]{1,0:T(8,128)S(1)}, f32[3,32,128]{2,1,0:T(8,128)S(1)}) custom-call(f32[81,64,128]{2,1,0:T(8,128)} %bitcast.12, f32[81,81]{1,0:T(8,128)} %base_hbm.1, f32[81,1025]{1,0:T(8,128)} %bitcast.13, bf16[3,32,128]{2,1,0:T(8,128)(2,1)} %bitcast.14, bf16[3,16,128]{2,1,0:T(8,128)(2,1)} %bitcast.15, f32[2,256,256]{2,1,0:T(8,128)} %constant.4.clone.mats_hbm, ...), custom_call_target="tpu_custom_call" | custom-call | tf_op jit(solution)/shard_map/pallas_call | solution.py:622
  74.3 1.6 %shard_map.150 = (f32[5184,128]{1,0:T(8,128)}, f32[3,32,128]{2,1,0:T(8,128)}) custom-call(f32[5184,128]{1,0:T(8,128)S(1)} %get-tuple-element.6.far, f32[3,32,128]{2,1,0:T(8,128)S(1)} %get-tuple-element.7.near), custom_call_target="tpu_custom_call" | custom-call | tf_op jit(solution)/shard_map/pallas_call | solution.py:675

commit v2 on v1

--- a/solution.py
+++ b/solution.py
@@ -124,18 +124,16 @@
 def decode(words, codes):
     rows = words.shape[0]
     lane = lax.broadcasted_iota(jnp.int32, (1, 128), 1)
-    diagonal = lax.broadcasted_iota(jnp.int32, (rows, 128), 0) == lax.broadcasted_iota(
-        jnp.int32, (rows, 128), 1
-    )
+    first = lax.broadcasted_iota(jnp.int32, (8, 128), 0) == 0
     c1 = (codes << 16) >> 16
     c0 = (codes - c1) >> 16
 
-    def column(code):
-        factor = jnp.exp2(code.astype(jnp.float32) * (0.5 / CODE)) * (1.0 / ROOT)
-        factor = jnp.where(lane < COMPS, factor, 0.0)
-        return jnp.sum(jnp.where(diagonal, factor, 0.0), axis=1, keepdims=True)
-
-    f0, f1 = column(c0), column(c1)
+    def factor(code):
+        found = jnp.exp2(code.astype(jnp.float32) * (0.5 / CODE)) * (1.0 / ROOT)
+        return jnp.broadcast_to(jnp.where(lane < COMPS, found, 0.0), (8, 128))
+
+    factors = jnp.transpose(jnp.where(first, factor(c0), factor(c1)))
+    f0, f1 = factors[0:rows, 0:1], factors[0:rows, 1:2]
     low = (words << 16) >> 16
     high = (words - low) >> 16
     return high.astype(jnp.float32) * f0 * f0, low.astype(jnp.float32) * f1 * f1
@@ -202,28 +200,28 @@
     slab = lax.axis_index("gx")
     lower, higher = lax.rem(slab + GX - 1, GX), lax.rem(slab + 1, GX)
 
+    barrier = pltpu.get_barrier_semaphore()
+
+    def greet(s, _):
+        pl.semaphore_signal(
+            barrier, inc=1, device_id={"gz": lax.rem(me + s, GZ)}, device_id_type=MESH
+        )
+        return 0
+
+    lax.fori_loop(1, GZ, greet, 0)
+    for side in (lower, higher):
+        pl.semaphore_signal(barrier, inc=1, device_id={"gx": side}, device_id_type=MESH)
+
     in_copies = [
         pltpu.make_async_copy(
             mult_hbm.at[:, pl.ds(c * 32, 32), :],
-            in_scr.reshape(ROWS, CELLS, PLANES).at[pl.ds(0, COMPS), pl.ds(c * 32, 32), :],
+            in_scr.reshape(ROWS + 1, CELLS, PLANES).at[pl.ds(0, COMPS), pl.ds(c * 32, 32), :],
             in_sem.at[c],
         )
         for c in range(2)
     ]
     for copy in in_copies:
         copy.start()
-    barrier = pltpu.get_barrier_semaphore()
-
-    def greet(s, _):
-        pl.semaphore_signal(
-            barrier, inc=1, device_id={"gz": lax.rem(me + s, GZ)}, device_id_type=MESH
-        )
-        return 0
-
-    lax.fori_loop(1, GZ, greet, 0)
-    for side in (lower, higher):
-        pl.semaphore_signal(barrier, inc=1, device_id={"gx": side}, device_id_type=MESH)
-
     par_copies = [
         pltpu.make_async_copy(src, dst, par_sem.at[i])
         for i, (src, dst) in enumerate(
@@ -247,8 +245,8 @@
     for copy in par_copies:
         copy.start()
 
-    in_scr[pl.ds(COMPS * CELLS, (ROWS - COMPS) * CELLS), :] = jnp.zeros(
-        ((ROWS - COMPS) * CELLS, PLANES), jnp.float32
+    in_scr[pl.ds(COMPS * CELLS, (ROWS + 1 - COMPS) * CELLS), :] = jnp.zeros(
+        ((ROWS + 1 - COMPS) * CELLS, PLANES), jnp.float32
     )
 
     def forward_words(c, peer):
@@ -268,12 +266,12 @@
             device_id_type=MESH,
         )
 
-    def copy_b(c, s, sender, receiver):
+    def copy_b(c, sender, receiver):
         return pltpu.make_async_remote_copy(
             src_ref=send_b.at[c, receiver, pl.ds(0, SENT)],
             dst_ref=recv_b.at[c, sender, pl.ds(0, SENT)],
-            send_sem=bs_sem.at[c, s],
-            recv_sem=br_sem.at[c, s],
+            send_sem=bs_sem.at[c, receiver],
+            recv_sem=br_sem.at[c, sender],
             device_id={"gz": receiver},
             device_id_type=MESH,
         )
@@ -310,7 +308,7 @@
         copy.wait()
     near_tx[...] = jnp.zeros_like(near_tx)
     for i in range(3):
-        leave_rows.reshape(POOL * 8, 128)[pl.ds(i, POOL, stride=8), :] = leave_off[i].astype(
+        leave_rows.reshape((POOL + 1) * 8, 128)[pl.ds(i, POOL, stride=8), :] = leave_off[i].astype(
             jnp.float32
         )
     lane = lax.broadcasted_iota(jnp.int32, (1, 128), 1)
@@ -528,15 +526,21 @@
             return encode(mixed[:, 0:128], mixed[:, 128:256])
 
         def answer(s, _):
-            peer = peer_after(s)
+            peer = peer_after(s + 1)
             words, codes = mixed_words(peer)
-            put(send_b, c, peer, words, codes)
-            copy_b(c, s, me, peer).start()
-            return 0
-
-        lax.fori_loop(1, GZ, answer, 0)
-        words, codes = mixed_words(me)
-        put(recv_b, c, me, words, codes)
+
+            @pl.when(peer == me)
+            def _():
+                put(recv_b, c, me, words, codes)
+
+            @pl.when(peer != me)
+            def _():
+                put(send_b, c, peer, words, codes)
+                copy_b(c, me, peer).start()
+
+            return 0
+
+        lax.fori_loop(0, GZ, answer, 0)
 
     def close_pencil(c, sender):
         words = recv_b[c, sender]
@@ -550,7 +554,7 @@
 
         def take(s, _):
             sender = peer_before(s)
-            copy_b(c, s, sender, me).wait_recv()
+            copy_b(c, sender, me).wait_recv()
             close_pencil(c, sender)
             return 0
 
@@ -565,7 +569,7 @@
     def drain(s, _):
         for c in range(2):
             copy_f(c, s, me, peer_after(s)).wait_send()
-            copy_b(c, s, me, peer_after(s)).wait_send()
+            copy_b(c, me, peer_after(s)).wait_send()
         return 0
 
     lax.fori_loop(1, GZ, drain, 0)
@@ -622,13 +626,13 @@
     taylors, near = pl.pallas_call(
         kernel,
         out_shape=(
-            pltpu.VMEM((COMPS * CELLS, PLANES), f32),
+            pltpu.VMEM(((COMPS + 1) * CELLS, PLANES), f32),
             pltpu.VMEM((3, BLK, 128), f32),
         ),
         in_specs=[hbm] * 14,
         out_specs=(vmem, vmem),
         scratch_shapes=[
-            pltpu.VMEM((ROWS * CELLS, PLANES), f32),
+            pltpu.VMEM(((ROWS + 1) * CELLS, PLANES), f32),
             pltpu.VMEM((2, GZ, ROWS, 128), i32),
             pltpu.VMEM((2, GZ, ROWS, 128), i32),
             pltpu.VMEM((2, GZ, ROWS, 128), i32),
@@ -653,10 +657,10 @@
             pltpu.SMEM((1, 1, POOL), f32),
             pltpu.SMEM((1, 1, 2, MAXB), i32),
             pltpu.SMEM((1, 1, 2), i32),
-            pltpu.VMEM((POOL, 8, 128), f32),
+            pltpu.VMEM((POOL + 1, 8, 128), f32),
             pltpu.VMEM(((BLK + 2) * 8, 128), f32),
             pltpu.VMEM((BLK + 2, 3, 8, 128), f32),
-            pltpu.VMEM((BLK * 8, 128), f32),
+            pltpu.VMEM(((BLK + 1) * 8, 128), f32),
             pltpu.VMEM((2, MAXB, 8, 128), f32),
             pltpu.VMEM((2 * MAXB, 8, 128), f32),
             dma((2,)),

time: 76 us -> 76.7 us (level)
  the two profiles are of different devices: /device:TPU:31 before, /device:TPU:62 now
where the time goes in v2:
time: 76.7 us; the launch traced here: 76.6 us
  Pallas kernels  75.9 us (99%)
    pallas_call x1, Pallas kernels, on_device(): pl.pallas_call(kernel, out_shape=(pltpu.VMEM(((COMPS + 1) * CELLS, PLANES...  74.4 us
    pallas_call x1, Pallas kernels, on_device(): pl.pallas_call(write_out, out_shape=(pltpu.HBM((COMPS * CELLS, PLANES), f...  1.6 us

profile of v2, /device:TPU:62, one launch (start us, length us, event | category | flops | bytes accessed | tf_op | source)
XLA Modules:
  0.0 76.6 jit_solution(13579104243889389735)
XLA Ops:
  0.6 74.4 %shard_map.149 = (f32[5248,128]{1,0:T(8,128)S(1)}, f32[3,32,128]{2,1,0:T(8,128)S(1)}) custom-call(f32[81,64,128]{2,1,0:T(8,128)} %bitcast.12, f32[81,81]{1,0:T(8,128)} %base_hbm.1, f32[81,1025]{1,0:T(8,128)} %bitcast.13, bf16[3,32,128]{2,1,0:T(8,128)(2,1)} %bitcast.14, bf16[3,16,128]{2,1,0:T(8,128)(2,1)} %bitcast.15, f32[2,256,256]{2,1,0:T(8,128)} %constant.4.clone.mats_hbm, ...), custom_call_target="tpu_custom_call" | custom-call | tf_op jit(solution)/shard_map/pallas_call | solution.py:626
  75.0 1.6 %shard_map.150 = (f32[5184,128]{1,0:T(8,128)}, f32[3,32,128]{2,1,0:T(8,128)}) custom-call(f32[5248,128]{1,0:T(8,128)S(1)} %get-tuple-element.6.far, f32[3,32,128]{2,1,0:T(8,128)S(1)} %get-tuple-element.7.near), custom_call_target="tpu_custom_call" | custom-call | tf_op jit(solution)/shard_map/pallas_call | solution.py:679
